TPU v7x, 32 devices: a whole 2x2x4 slice. The times are simulated.
32 devices in a mesh: grp: 2 (over y), slab: 4 (over z), ang: 2 (over x), rep: 2 (over core).
Axes of the slice: x: 2, y: 2, z: 4, core: 2. Of those that a mesh axis runs over, the one named last changes fastest.
Arguments:
- volume: float32 [64, 512], P(('grp', 'slab'), 'rep'), parts along dimension 0, may hold values from 0.5 to 2
- measured: float32 [32, 8, 2048], P(('grp', 'ang'), None, 'slab'), parts along dimension 0, may hold values from 0.5 to 8
- in_plane: bfloat16 [16, 4, 512, 2048], P('ang', 'slab', 'rep'), may hold values from 0.0009994507 to 0.0099487305
- pair_bands: int32 [16, 4, 5], P('ang', 'slab'), may hold values from 0 to 3, as said below
- pair_counts: int32 [16, 4], P('ang', 'slab'), may hold values from 2 to 4, as said below
- pair_weight_tiles: float32 [16, 4, 5, 2, 8], P('ang', 'slab'), may hold values from 0.01 to 0.1
Outputs:
- new_volume: float32 [64, 512], P(('grp', 'slab'), 'rep'), parts along dimension 0
- residual: float32 [32, 8, 2048], P(('grp', 'ang'), ('slab', 'rep')), parts along dimension 0
There are 2 independent parts, one for each index of `grp`. A program takes and returns all parts, laid end to end along the dimension named above; an argument that names none is the same for every part. Nothing has to cross between parts.
Inputs may be any that keep to these rules, and one draw needn't show every extreme that they name: `pair_bands`: for angle a and slab s the first pair_counts[a, s] entries are the consecutive bands from max(0, s - h) to min(3, s + h) in increasing order, for some h of 1 to 2; the other entries are 0. Every band is listed by its own slab. `pair_counts`: the length of each list as described for pair_bands.
All inputs are finite; a program needn't handle non-finite values.
Results may differ from a plain program's by a relative error of at most 0.0003.
Values may be sent and summed in bfloat16 or wider, within the bound.
A program may use at most 64 MiB of HBM per device.

v0:
```python
import jax
import jax.numpy as jnp
from jax import lax
from jax.sharding import PartitionSpec as P


def body(volume, measured, in_plane, pair_bands, pair_counts, pair_weight_tiles):
    largest_index = lax.Precision.HIGHEST
    slabs = lax.axis_size("slab")
    angles = in_plane.shape[0]
    width_u = in_plane.shape[3]
    rows_band = pair_weight_tiles.shape[3]
    slot_count = pair_weight_tiles.shape[2]
    footprint = in_plane[:, 0]
    tiles_here = pair_weight_tiles[:, 0]
    band_ids = pair_bands[:, 0]
    active_slot = jnp.arange(slot_count, dtype=jnp.int32)[None, :] < pair_counts
    volume_copy = volume.astype(jnp.bfloat16)
    plane_proj = jnp.einsum(
        "zx,axu->azu", volume_copy, footprint, preferred_element_type=jnp.float32
    )
    plane_ones = jnp.sum(footprint, axis=1, dtype=jnp.float32)
    voxel_rays = jnp.sum(footprint, axis=2, dtype=jnp.float32)
    picked_blocks = (
        (band_ids[:, :, None] == jnp.arange(slabs, dtype=jnp.int32)[None, None, :])
        & active_slot[:, :, None]
    ).astype(jnp.float32)
    tile_lookup = jnp.einsum("acd,acrz->adrz", picked_blocks, tiles_here, precision=largest_index)
    band_weight = jnp.sum(tile_lookup, axis=3)
    band_panel = lax.all_to_all(measured, "slab", split_axis=1, concat_axis=2, tiled=True)
    half_rows = rows_band // 2
    rep_start = lax.axis_index("rep") * half_rows
    proj_terms = jnp.einsum(
        "adrz,azu->adru", tile_lookup, plane_proj, precision=largest_index
    ).reshape(angles, slabs * rows_band, width_u)
    ones_terms = jnp.einsum(
        "adr,au->adru", band_weight, plane_ones, precision=largest_index
    ).reshape(angles, slabs * rows_band, width_u)
    forward, ray_sums = (
        lax.psum_scatter(proj_terms, ("slab", "rep"), scatter_dimension=1, tiled=True),
        lax.psum_scatter(ones_terms, ("slab", "rep"), scatter_dimension=1, tiled=True),
    )
    own_rows = lax.dynamic_slice_in_dim(band_panel, rep_start, half_rows, 1)
    residual = (own_rows - forward) / ray_sums
    residual_b = residual.astype(jnp.bfloat16)
    gathered = lax.all_gather(residual_b, ("slab", "rep"), axis=1, tiled=True)
    gathered = gathered.reshape(angles, slabs, rows_band, width_u)
    back_rows = jnp.einsum(
        "adrz,adru->azu", tile_lookup, gathered.astype(jnp.float32), precision=largest_index
    )
    back_b = back_rows.astype(jnp.bfloat16)
    update = jnp.einsum("azu,axu->zx", back_b, footprint, preferred_element_type=jnp.float32)
    voxel_sums = jnp.einsum(
        "az,ax->zx", jnp.sum(tile_lookup, axis=(1, 2)), voxel_rays, precision=largest_index
    )
    update, voxel_sums = lax.psum((update, voxel_sums), "ang")
    new_volume = volume + update / voxel_sums
    return (new_volume, residual)


def solution(mesh):
    return jax.shard_map(
        body,
        mesh=mesh,
        in_specs=(
            P(("grp", "slab"), "rep"),
            P(("grp", "ang"), None, "slab"),
            P("ang", "slab", "rep", None),
            P("ang", "slab", None),
            P("ang", "slab"),
            P("ang", "slab", None, None, None),
        ),
        out_specs=(P(("grp", "slab"), "rep"), P(("grp", "ang"), ("slab", "rep"), None)),
        check_vma=False,
    )
```

profile of v0, /device:TPU:0, one launch (start us, length us, event | category | flops | bytes accessed | tf_op | source)
XLA Modules:
  0.0 119.4 jit_solution(2195852654092383292)
XLA Ops:
  7.2 0.0 copy-start
  7.2 0.0 reduce-scatter.3.cloned.1.call-start
  7.2 0.8 copy.23
  8.0 0.7 iota_compare_fusion.1
  8.7 5.3 %fusion.4 = f32[8,2048,8,1]{1,2,3,0:T(8,128)S(1)} fusion(bf16[8,1,256,2048]{3,2,1,0:T(8,128)(2,1)} %param.8, f32[8,256]{1,0:T(8,128)} %param.6), kind=kOutput, calls=%fused_computation.6 | convolution fusion | flops 67110912 | bytes 8921088 | tf_op jit(solution)/shard_map/zx,axu->azu/dot_general | solution.py:19
  14.1 0.0 copy-start.1
  14.1 0.0 copy-done
  14.1 0.3 fusion.21
  14.3 0.7 fusion.23
  15.0 1.1 copy.27
  16.1 0.0 reduce-scatter.3.cloned.1.call-update
  16.1 0.0 reduce-scatter.5.cloned.1.call-start
  16.2 0.1 copy.28
  16.3 0.0 copy-start.2
  16.3 6.1 %convert_reduce_fusion = (f32[8,256]{1,0:T(8,128)S(1)}, f32[8,2048]{1,0:T(8,128)S(1)}) fusion(bf16[8,1,256,2048]{3,2,1,0:T(8,128)(2,1)} %param.8), kind=kLoop, calls=%fused_computation | loop fusion | flops 12564480 | bytes 8462336 | tf_op jit(solution)/shard_map/reduce_sum | solution.py:23
  22.4 0.9 broadcast_multiply_fusion
  23.3 0.0 reduce-scatter.5.cloned.1.call-update
  23.3 0.0 copy-done.1
  23.3 0.7 copy.25
  24.0 6.3 %all-to-all-start = ((f32[8,8,512]{2,0,1:T(8,128)}), f32[8,8,512]{2,0,1:T(8,128)S(1)}, u32[]{:S(2)}, u32[]{:S(2)}) async-start(f32[8,8,512]{2,0,1:T(8,128)} %copy.25), calls=%async_computation | async-start | bytes 262144 | tf_op jit(solution)/shard_map/all_to_all | solution.py:30
  30.4 0.2 fusion.24
  30.5 7.0 %all-to-all-done = f32[8,8,512]{2,0,1:T(8,128)S(1)} async-done(((f32[8,8,512]{2,0,1:T(8,128)}), f32[8,8,512]{2,0,1:T(8,128)S(1)}, u32[]{:S(2)}, u32[]{:S(2)}) %all-to-all-start) | async-done | bytes 131104 | tf_op jit(solution)/shard_map/all_to_all | solution.py:30
  37.6 12.4 %reduce-scatter.3.cloned.1.call-done = f32[8,1,2048]{2,0,1:T(8,128)} async-done(((f32[8,8,2048]{2,0,1:T(8,128)}), f32[8,1,2048]{2,0,1:T(8,128)}) %reduce-scatter.3.cloned.1.call-update) | async-done | bytes 65552 | tf_op jit(solution)/shard_map/reduce_scatter | solution.py:40
  50.0 31.8 %reduce-scatter.5.cloned.1.call-done = f32[8,1,2048]{2,0,1:T(8,128)} async-done(((f32[8,8,2048]{2,0,1:T(8,128)}), f32[8,1,2048]{2,0,1:T(8,128)}) %reduce-scatter.5.cloned.1.call-update) | async-done | bytes 65552 | tf_op jit(solution)/shard_map/reduce_scatter | solution.py:41
  81.8 0.9 fusion.22
  82.7 14.2 %all_gather.3 = bf16[8,8,2048]{2,0,1:T(8,128)(2,1)S(1)} all-gather(bf16[8,1,2048]{2,0,1:T(8,128)(2,1)S(1)} %get-tuple-element.14), channel_id=1, replica_groups=mesh['grp'=2,'slab'=4,'ang'=2,'rep'=2] {'slab','rep'}, dimensions={1}, use_global_device_ids=true | all-gather | bytes 294912 | tf_op jit(solution)/shard_map/all_gather | solution.py:46
  96.9 0.6 fusion.7
  97.5 5.6 %fusion.8 = f32[8,256]{1,0:T(8,128)S(1)} fusion(bf16[8,8,2048]{2,1,0:T(8,128)(2,1)S(1)} %fusion.7, bf16[8,1,256,2048]{3,2,1,0:T(8,128)(2,1)} %param.8), kind=kOutput, calls=%fused_computation.9 | convolution fusion | flops 67108864 | bytes 8658944 | tf_op jit(solution)/shard_map/azu,axu->zx/dot_general | solution.py:52
  103.2 0.7 copy.30
  103.9 8.1 %all-reduce = (f32[8,256]{1,0:T(8,128)S(1)}, f32[8,256]{1,0:T(8,128)S(1)}) all-reduce(f32[8,256]{1,0:T(8,128)S(1)} %fusion.8, f32[8,256]{1,0:T(8,128)S(1)} %fusion.24), channel_id=1, replica_groups=mesh['grp'=2,'slab'=4,'ang'=2,'rep'=2] {'ang'}, use_global_device_ids=true, to_apply=%region_4.0 | all-reduce | flops 4096 | bytes 32768 | tf_op jit(solution)/shard_map/psum | solution.py:56
  112.0 0.0 copy-done.2
  112.0 0.6 divide_add_fusion
  (1 shorter events, 0.0 us)
Async XLA Ops:
  7.2 6.9 %copy-start = (f32[8,1,5,2,8]{4,3,2,1,0:T(2,128)S(1)}, f32[8,1,5,2,8]{4,3,2,1,0:T(2,128)}, u32[]{:S(2)}) copy-start(f32[8,1,5,2,8]{4,3,2,1,0:T(2,128)} %param.11) | copy-start | bytes 7684
  7.2 42.9 %reduce-scatter.3.cloned.1.call-start = ((), (), s32[]{:S(2)}) async-start(), calls=%async_computation.3 | async-start | bytes 589824 | tf_op jit(solution)/shard_map/reduce_scatter | solution.py:40
  14.1 9.2 %copy-start.1 = (f32[8,8,512]{2,1,0:T(8,128)S(1)}, f32[8,8,512]{2,1,0:T(8,128)}, u32[]{:S(2)}) copy-start(f32[8,8,512]{2,1,0:T(8,128)} %param.7) | copy-start | bytes 393220
  16.1 65.7 %reduce-scatter.5.cloned.1.call-start = ((), (), s32[]{:S(2)}) async-start(), calls=%async_computation.4 | async-start | bytes 589824 | tf_op jit(solution)/shard_map/reduce_scatter | solution.py:41
  16.3 95.7 %copy-start.2 = (f32[8,256]{1,0:T(8,128)S(1)}, f32[8,256]{1,0:T(8,128)}, u32[]{:S(2)}) copy-start(f32[8,256]{1,0:T(8,128)} %param.6) | copy-start | bytes 24580
  24.0 13.5 %all-to-all-start = ((f32[8,8,512]{2,0,1:T(8,128)}), f32[8,8,512]{2,0,1:T(8,128)S(1)}, u32[]{:S(2)}, u32[]{:S(2)}) async-start(f32[8,8,512]{2,0,1:T(8,128)} %copy.25), calls=%async_computation | async-start | bytes 262144 | tf_op jit(solution)/shard_map/all_to_all | solution.py:30
Sparse Core Ops, SparseCore 0:
  16.3 33.7 reduce-scatter.2
  52.4 29.3 reduce-scatter.4
where the time goes:
time: 120 us; the launch traced here: 119 us
  waiting for transfers between devices  51.3 us (43%)
  blocking collectives  22.3 us (19%)
  between operations  14.1 us (12%)
  matrix products  12.7 us (11%)
  other arithmetic  9.23 us (8%)
  starting transfers between devices  6.4 us (5%)
  local copies, waits for them, and re-layouts  3.41 us (3%)
    reduce_scatter x1, waiting for transfers between devices, body(): lax.psum_scatter(ones_terms, ('slab', 'rep'), scatter_dimension=1, tiled=...  31.8 us
    all_gather x1, blocking collectives, body(): gathered = lax.all_gather(residual_b, ('slab', 'rep'), axis=1, tiled=True)  14.2 us
    reduce_scatter x1, waiting for transfers between devices, body(): lax.psum_scatter(proj_terms, ('slab', 'rep'), scatter_dimension=1, tiled=...  12.4 us
    psum x1, blocking collectives, body(): update, voxel_sums = lax.psum((update, voxel_sums), 'ang')  8.13 us
    all_to_all x1, waiting for transfers between devices, body(): lax.all_to_all(measured, 'slab', split_axis=1, concat_axis=2, tiled=True)  7.04 us
    all_to_all x1, starting transfers between devices, body(): lax.all_to_all(measured, 'slab', split_axis=1, concat_axis=2, tiled=True)  6.32 us
    reduce_sum x1, other arithmetic, body(): voxel_rays = jnp.sum(footprint, axis=2, dtype=jnp.float32)  6.08 us
    dot_general x1, matrix products, body(): jnp.einsum('azu,axu->zx', back_b, footprint, preferred_element_type=jnp.f...  5.64 us
  transfers between devices with their start and end apart: 3, of which 3 were waited for; matrix products, arithmetic and copies ran while one was open for 7% of the time, Pallas kernels for 0%

commit v1 on v0

v1 whole, which is shorter than its diff:
```python
import functools

import jax
import jax.numpy as jnp
from jax import lax
from jax.experimental import pallas as pl
from jax.experimental.pallas import tpu as pltpu
from jax.sharding import PartitionSpec as P

MESH = pl.DeviceIdType.MESH
F32 = jnp.float32
BF16 = jnp.bfloat16
EXACT = lax.Precision.HIGHEST
LANES = 128
ROWS = 8
WEIGHT_MAX = 0.0099487305
VOLUME_MAX = 2.0
HALF_CODE = 32500.0
CHUNKS = 4


def each(count, fn):
    if count <= 8:
        for i in range(count):
            fn(i)
    else:
        pl.loop(0, count)(fn)


def kernel(
    cfg,
    volume, measured, in_plane, bands, counts, tiles,
    new_volume, residual,
    wide, rows_t, bd_raw, bd_mean, tw, proj,
    meas_send, meas_recv, half_own, half_send, half_recv,
    code_send, code_recv, gather, res_all, res_wide, acc, x_send, x_recv,
    w_sem, ms_s, ms_r, f_s, f_r, q_s, q_r, r_s, r_r, p_s, p_r, x_s, x_r,
):
    slabs, angs, span, angles, zs, cw, chunks, strip = cfg
    me = lax.axis_index("slab")
    rep = lax.axis_index("rep")
    ang = lax.axis_index("ang")
    other = 1 - rep
    nrow = slabs * ROWS
    nz = angles * zs
    xy = volume.shape[1]
    xy_all = 2 * xy
    mean_scale = 2 * HALF_CODE / (xy_all * VOLUME_MAX * WEIGHT_MAX * 1.001)
    ones_scale = 2 * HALF_CODE / (xy_all * WEIGHT_MAX * 1.001)

    def cols(k):
        return pl.ds(k * cw, cw)

    def block(d):
        return pl.ds(pl.multiple_of(d * ROWS, ROWS), ROWS)

    def load(k):
        return pltpu.make_async_copy(in_plane.at[:, 0, :, cols(k)], wide.at[k], w_sem.at[k])

    def remote(src, dst, s, r, to):
        return pltpu.make_async_remote_copy(
            src_ref=src, dst_ref=dst, send_sem=s, recv_sem=r, device_id=to, device_id_type=MESH
        )

    def meas_copy(d, slot):
        return remote(meas_send.at[d], meas_recv.at[slot], ms_s.at[d], ms_r.at[slot], {"slab": d})

    def half_copy(k):
        return remote(half_send.at[k], half_recv.at[k], f_s.at[k], f_r.at[k], {"rep": other})

    def code_copy(k, d, slot):
        return remote(code_send.at[k, d], code_recv.at[k, slot], q_s.at[k, d], q_r.at[k, slot], {"slab": d})

    def res_copy(k, d, slot):
        src = gather.at[k, 0, me]
        return remote(src, gather.at[k, 0, slot], r_s.at[k, d], r_r.at[k, slot], {"slab": d})

    def pass_copy(k, s):
        return remote(gather.at[k, 0, s], gather.at[k, 1, s], p_s.at[k, s], p_r.at[k, s], {"rep": other})

    def x_copy(to, slot):
        return remote(x_send, x_recv.at[slot], x_s.at[to], x_r.at[slot], {"ang": to})

    def near(fn):
        def one(i):
            d = me + (span - i // 2) * (1 - 2 * (i % 2))

            @pl.when((d >= 0) & (d < slabs))
            def _():
                fn(d)

        each(2 * span, one)

    def others(count, mine, fn):
        each(count - 1, lambda i: fn(lax.rem(mine + i + 1, count)))

    for k in range(chunks):
        load(k).start()

    if angles < ROWS:
        meas_send[...] = jnp.zeros_like(meas_send)
        half_own[...] = jnp.zeros_like(half_own)
        half_send[...] = jnp.zeros_like(half_send)
    rows_t[...] = jnp.zeros_like(rows_t)
    gather[...] = jnp.zeros_like(gather)

    barrier = pltpu.get_barrier_semaphore()
    others(slabs, me, lambda d: pl.semaphore_signal(barrier, inc=1, device_id={"slab": d}, device_id_type=MESH))
    others(angs, ang, lambda d: pl.semaphore_signal(barrier, inc=1, device_id={"ang": d}, device_id_type=MESH))
    pl.semaphore_signal(barrier, inc=1, device_id={"rep": other}, device_id_type=MESH)

    def fill(d):
        for a in range(angles):
            meas_send[d, a : a + 1, LANES : LANES + strip] = measured[a, pl.ds(d * 2 + rep, 1), :]
            first = bands[a, 0, 0]
            count = counts[a, 0]
            listed = jnp.where((d >= first) & (d < first + count), F32(1), F32(0))
            slot = jnp.clip(d - first, 0, tiles.shape[2] - 1)
            rows_t[0, d, a : a + 1, 0:zs] = tiles[a, 0, slot, pl.ds(rep, 1), :] * listed
            rows_t[1, d, a : a + 1, 0:zs] = tiles[a, 0, slot, pl.ds(other, 1), :] * listed

    each(slabs, fill)

    lane = lax.broadcasted_iota(jnp.int32, (ROWS, LANES), 1)
    row = lax.broadcasted_iota(jnp.int32, (ROWS, LANES), 0)
    same = (lane // zs) == row

    def blocks(d):
        for r in range(2):
            y = rows_t[r, d]
            weight = jnp.sum(y, axis=1, keepdims=True)
            if r == 0:
                meas_send[d, :, 0:LANES] = jnp.broadcast_to(weight, (ROWS, LANES))
            width = zs
            while width < nz:
                y = y + pltpu.roll(y, width, 1)
                width *= 2
            y = jnp.where(same, y, 0.0)[:, :nz]
            at = block(r * slabs + d)
            bd_raw[at, :] = y
            bd_mean[at, :] = y * (mean_scale / jnp.maximum(weight, 1e-30))

    each(slabs, blocks)
    pl.semaphore_wait(barrier, slabs + angs - 1)
    others(slabs, me, lambda d: meas_copy(d, me).start())

    tw[...] = lax.dot_general(
        bd_raw[...], jnp.ones((2 * nrow, LANES), F32), (((0,), (0,)), ((), ())),
        precision=EXACT, preferred_element_type=F32,
    )
    acc[...] = jnp.zeros_like(acc)
    left = jnp.concatenate([volume[...], jnp.ones_like(volume)], axis=0).astype(BF16)

    def project(k):
        load(k).wait()
        for a in range(angles):
            got = jnp.dot(left, wide[k, a], preferred_element_type=F32)
            proj[a * zs : (a + 1) * zs, :] = got[0:zs]
            half_own[k, nrow + a : nrow + a + 1, :] = got[zs : zs + 1]
            half_send[k, nrow + a : nrow + a + 1, :] = got[zs : zs + 1]
        mix = jnp.dot(bd_mean[...], proj[...], precision=EXACT, preferred_element_type=F32)
        half_own[k, 0:nrow, :] = mix[0:nrow]
        half_send[k, 0:nrow, :] = mix[nrow:]
        half_copy(k).start()

    def scatter(k):
        half_copy(k).wait_recv()
        ones = half_own[k, nrow:, :] + half_recv[k, nrow:, :]
        ones_code = jnp.round(ones * ones_scale - HALF_CODE)

        def send(d):
            mean = half_own[k, block(d), :] + half_recv[k, block(d), :]
            code = jnp.concatenate([jnp.round(mean - HALF_CODE), ones_code], axis=0)
            code_send[k, d] = code.astype(jnp.int32).astype(jnp.int16)
            code_copy(k, d, me).start()

        near(send)

    def wide_weight(s):
        return jnp.concatenate([meas_recv[s, :, 0:LANES]] * (cw // LANES), axis=1)

    def own_weight():
        return jnp.concatenate([meas_send[me, :, 0:LANES]] * (cw // LANES), axis=1)

    def solve(k):
        if k == 0:
            others(slabs, me, lambda s: meas_copy(s, s).wait_recv())
            meas_recv[me] = meas_send[me]
        weight = own_weight()
        res_wide[0:ROWS, :] = weight * (half_own[k, block(me), :] + half_recv[k, block(me), :])
        res_wide[ROWS:, :] = weight * ((half_own[k, nrow:, :] + half_recv[k, nrow:, :]) * ones_scale)

        def add(s):
            code_copy(k, s, s).wait_recv()
            code = code_recv[k, s].astype(jnp.int32).astype(F32) + HALF_CODE
            weight = wide_weight(s)
            res_wide[0:ROWS, :] += weight * code[0:ROWS]
            res_wide[ROWS:, :] += weight * code[ROWS:]

        near(add)
        if strip <= cw:
            each_k = cw // strip
            row_meas = jnp.concatenate(
                [meas_recv[k * each_k + j, :, LANES : LANES + strip] for j in range(each_k)], axis=1
            )
        else:
            start = (k * cw) % strip
            row_meas = meas_recv[(k * cw) // strip, :, LANES + start : LANES + start + cw]
        res = (row_meas - res_wide[0:ROWS, :] * (1.0 / mean_scale)) / (res_wide[ROWS:, :] * (1.0 / ones_scale))
        if angles < ROWS:
            res = jnp.where(lax.broadcasted_iota(jnp.int32, res.shape, 0) < angles, res, 0.0)
        residual[:, cols(k)] = res[0:angles]
        gather[k, 0, me] = jnp.concatenate([res[:, : cw // 2], res[:, cw // 2 :]], axis=0).astype(BF16)
        near(lambda d: res_copy(k, d, me).start())
        pass_copy(k, me).start()

    def relay(k):
        def one(s):
            res_copy(k, s, s).wait_recv()
            pass_copy(k, s).start()

        near(one)

    def back(k):
        near(lambda s: pass_copy(k, s).wait_recv())
        pass_copy(k, me).wait_recv()
        for r in range(2):

            def spread(d):
                got = gather[k, r, d].astype(F32)
                at = block(r * slabs + d)
                res_all[at, : cw // 2] = got[0:ROWS]
                res_all[at, cw // 2 :] = got[ROWS:]

            each(slabs, spread)
        rows_back = lax.dot_general(
            bd_raw[...], res_all[...], (((0,), (0,)), ((), ())), precision=EXACT, preferred_element_type=F32
        )
        update = acc[0:zs, :]
        sums = acc[zs:, :]
        ones = jnp.ones((zs, cw), F32)
        for a in range(angles):
            lhs = jnp.concatenate([rows_back[a * zs : (a + 1) * zs], ones], axis=0).astype(BF16)
            got = lax.dot_general(lhs, wide[k, a], (((1,), (1,)), ((), ())), preferred_element_type=F32)
            update = update + got[0:zs]
            weight = jnp.concatenate([tw[a * zs : (a + 1) * zs, :]] * (xy // LANES), axis=1)
            sums = sums + weight * got[zs:]
        acc[0:zs, :] = update
        acc[zs:, :] = sums

    stages = (project, scatter, solve, relay, back)
    lags = (0, 1, 2, 3, 4)
    for step in range(chunks + lags[-1]):
        for stage, lag in zip(stages, lags):
            if 0 <= step - lag < chunks:
                stage(step - lag)

    x_send[...] = acc[...]
    others(angs, ang, lambda to: x_copy(to, ang).start())
    others(angs, ang, lambda s: x_copy(s, s).wait_recv())
    x_recv[ang] = x_send[...]
    total = x_recv[0]
    for i in range(1, angs):
        total = total + x_recv[i]
    new_volume[...] = volume[...] + total[0:zs] / total[zs:]

    others(slabs, me, lambda d: meas_copy(d, me).wait_send())
    others(angs, ang, lambda to: x_copy(to, ang).wait_send())
    for k in range(chunks):
        half_copy(k).wait_send()
        pass_copy(k, me).wait_send()

        def done(d):
            code_copy(k, d, me).wait_send()
            res_copy(k, d, me).wait_send()
            pass_copy(k, d).wait_send()

        near(done)


def body(mesh, volume, measured, in_plane, pair_bands, pair_counts, pair_weight_tiles):
    slabs, angs = mesh.shape["slab"], mesh.shape["ang"]
    angles, _, xy, width = in_plane.shape
    zs = volume.shape[0]
    span = (pair_weight_tiles.shape[2] - 1) // 2
    chunks = CHUNKS
    cw = width // chunks
    strip = measured.shape[2]
    cfg = (slabs, angs, span, angles, zs, cw, chunks, strip)
    nrow, nz = slabs * ROWS, angles * zs
    dma = pltpu.SemaphoreType.DMA
    vmem = pl.BlockSpec(memory_space=pltpu.VMEM)
    smem = pl.BlockSpec(memory_space=pltpu.SMEM)
    new_volume, residual = pl.pallas_call(
        functools.partial(kernel, cfg),
        out_shape=(
            jax.ShapeDtypeStruct((zs, xy), F32),
            jax.ShapeDtypeStruct((angles, width), F32),
        ),
        in_specs=[vmem, vmem, pl.BlockSpec(memory_space=pl.ANY), smem, smem, vmem],
        out_specs=(vmem, vmem),
        scratch_shapes=[
            pltpu.VMEM((chunks, angles, xy, cw), BF16),
            pltpu.VMEM((2, slabs, ROWS, LANES), F32),
            pltpu.VMEM((2 * nrow, nz), F32),
            pltpu.VMEM((2 * nrow, nz), F32),
            pltpu.VMEM((nz, LANES), F32),
            pltpu.VMEM((nz, cw), F32),
            pltpu.VMEM((slabs, ROWS, LANES + strip), F32),
            pltpu.VMEM((slabs, ROWS, LANES + strip), F32),
            pltpu.VMEM((chunks, nrow + ROWS, cw), F32),
            pltpu.VMEM((chunks, nrow + ROWS, cw), F32),
            pltpu.VMEM((chunks, nrow + ROWS, cw), F32),
            pltpu.VMEM((chunks, slabs, 2 * ROWS, cw), jnp.int16),
            pltpu.VMEM((chunks, slabs, 2 * ROWS, cw), jnp.int16),
            pltpu.VMEM((chunks, 2, slabs, 2 * ROWS, cw // 2), BF16),
            pltpu.VMEM((2 * nrow, cw), F32),
            pltpu.VMEM((2 * ROWS, cw), F32),
            pltpu.VMEM((2 * zs, xy), F32),
            pltpu.VMEM((2 * zs, xy), F32),
            pltpu.VMEM((angs, 2 * zs, xy), F32),
            dma((chunks,)),
            dma((slabs,)), dma((slabs,)),
            dma((chunks,)), dma((chunks,)),
            dma((chunks, slabs)), dma((chunks, slabs)),
            dma((chunks, slabs)), dma((chunks, slabs)),
            dma((chunks, slabs)), dma((chunks, slabs)),
            dma((angs,)), dma((angs,)),
        ],
        compiler_params=pltpu.CompilerParams(
            collective_id=0, has_side_effects=True, vmem_limit_bytes=40 * 1024 * 1024
        ),
        cost_estimate=pl.CostEstimate(
            flops=8 * angles * zs * xy * width, bytes_accessed=2 * angles * xy * width, transcendentals=0
        ),
    )(volume, measured, in_plane, pair_bands, pair_counts, pair_weight_tiles)
    return new_volume, residual.reshape(angles, 1, width)


def solution(mesh):
    return jax.shard_map(
        functools.partial(body, mesh),
        mesh=mesh,
        in_specs=(
            P(("grp", "slab"), "rep"),
            P(("grp", "ang"), None, "slab"),
            P("ang", "slab", "rep", None),
            P("ang", "slab", None),
            P("ang", "slab"),
            P("ang", "slab", None, None, None),
        ),
        out_specs=(P(("grp", "slab"), "rep"), P(("grp", "ang"), ("slab", "rep"), None)),
        check_vma=False,
    )
```

time: 120 us -> 37.5 us (0.31)
  waiting for transfers between devices: 51.3 us -> 0 us
  Pallas kernels: 0 us -> 28 us
  blocking collectives: 22.3 us -> 0 us
  between operations: 14.1 us -> 0.64 us
  matrix products: 12.7 us -> 0 us
  other arithmetic: 9.23 us -> 0 us
  starting transfers between devices: 6.4 us -> 0 us
  local copies, waits for them, and re-layouts: 3.41 us -> 8.54 us
    reduce_scatter x2 -> x0, waiting for transfers between devices: 44.2 us -> none  [the longest x1 31.8 us: body(): lax.psum_scatter(ones_terms, ('slab', 'rep'), scatter_dimension=1, tiled=...]
    pallas_call x0 -> x1, Pallas kernels: none -> 28 us  [body(): pl.pallas_call(functools.partial(kernel, cfg), out_shape=(jax.ShapeDtypeS...]
    all_gather x1 -> x0, blocking collectives: 14.2 us -> none  [body(): gathered = lax.all_gather(residual_b, ('slab', 'rep'), axis=1, tiled=True)]
    dot_general x6 -> x0, matrix products: 12.7 us -> none  [the longest x1 5.64 us: body(): jnp.einsum('azu,axu->zx', back_b, footprint, preferred_element_type=jnp.f...]
    psum x1 -> x0, blocking collectives: 8.13 us -> none  [body(): update, voxel_sums = lax.psum((update, voxel_sums), 'ang')]
    all_to_all x1 -> x0, waiting for transfers between devices: 7.04 us -> none  [body(): lax.all_to_all(measured, 'slab', split_axis=1, concat_axis=2, tiled=True)]
    unnamed x9 -> x12, local copies, waits for them, and re-layouts: 2.22 us -> 8.54 us
    all_to_all x1 -> x0, starting transfers between devices: 6.32 us -> none  [body(): lax.all_to_all(measured, 'slab', split_axis=1, concat_axis=2, tiled=True)]
  transfers between devices with their start and end apart: 3 -> 0, of which waited for: 3 -> 0; matrix products, arithmetic and copies ran while one was open for 7% -> 0% of each run, Pallas kernels for 0% -> 0%
where the time goes in v1:
time: 37.5 us; the launch traced here: 37.2 us
  Pallas kernels  28 us (75%)
  local copies, waits for them, and re-layouts  8.54 us (23%)
  between operations  0.64 us (2%)
    pallas_call x1, Pallas kernels, body(): pl.pallas_call(functools.partial(kernel, cfg), out_shape=(jax.ShapeDtypeS...  28 us
    unnamed x12, local copies, waits for them, and re-layouts  8.54 us

profile of v1, /device:TPU:0, one launch (start us, length us, event | category | flops | bytes accessed | tf_op | source)
XLA Modules:
  0.0 37.2 jit_solution(13048804459022394336)
XLA Ops:
  0.6 0.8 %copy.8.bands = s32[8,1,5]{2,1,0:T(1,128)S(1)} copy(s32[8,1,5]{0,1,2:T(1,128)} %param.9) | data formatting | bytes 320 | tf_op args[3]
  1.4 0.7 %copy.9.counts = s32[8,1]{1,0:T(8,128)S(1)} copy(s32[8,1]{0,1:T(1,128)} %param.10) | data formatting | bytes 64 | tf_op args[4]
  2.1 0.0 copy-start
  2.1 3.4 %copy-done = bf16[8,1,256,2048]{3,2,1,0:T(8,128)(2,1)S(1)} copy-done((bf16[8,1,256,2048]{3,2,1,0:T(8,128)(2,1)S(1)}, bf16[8,1,256,2048]{3,2,1,0:T(8,128)(2,1)}, u32[]{:S(2)}) %copy-start) | copy-done | bytes 8388632
  5.5 0.0 copy-start.1
  5.5 0.9 %copy-done.1 = f32[8,8,512]{2,1,0:T(8,128)S(1)} copy-done((f32[8,8,512]{2,1,0:T(8,128)S(1)}, f32[8,8,512]{2,1,0:T(8,128)}, u32[]{:S(2)}) %copy-start.1) | copy-done | bytes 131096
  6.4 0.0 copy-start.2
  6.4 0.8 %copy-done.2 = f32[8,1,5,2,8]{4,3,2,1,0:T(2,128)S(1)} copy-done((f32[8,1,5,2,8]{4,3,2,1,0:T(2,128)S(1)}, f32[8,1,5,2,8]{4,3,2,1,0:T(2,128)}, u32[]{:S(2)}) %copy-start.2) | copy-done | bytes 2584
  7.2 0.0 copy-start.3
  7.2 0.7 %copy-done.3 = f32[8,256]{1,0:T(8,128)S(1)} copy-done((f32[8,256]{1,0:T(8,128)S(1)}, f32[8,256]{1,0:T(8,128)}, u32[]{:S(2)}) %copy-start.3) | copy-done | bytes 8216
  7.9 28.0 %shard_map.77 = (f32[8,256]{1,0:T(8,128)S(1)}, f32[8,2048]{1,0:T(8,128)S(1)}) custom-call(f32[8,256]{1,0:T(8,128)S(1)} %copy-done.3, f32[8,8,512]{2,1,0:T(8,128)S(1)} %copy-done.1, bf16[8,1,256,2048]{3,2,1,0:T(8,128)(2,1)S(1)} %copy-done, s32[8,1,5]{2,1,0:T(1,128)S(1)} %copy.8.bands, s32[8,1]{1,0:T(8,128)S(1)} %copy.9.counts, f32[8,1,5,2,8]{4,3,2,1,0:T(2,128)S(1)} %copy-done.2), custom_call_target="tpu_custom_call" | custom-call | flops 268435456 | bytes 8388608 | tf_op jit(solution)/shard_map/pallas_call | solution.py:294
  35.9 0.7 %copy.10 = f32[8,1,2048]{2,1,0:T(1,128)} copy(f32[8,1,2048]{2,0,1:T(8,128)S(1)} %bitcast.1) | data formatting | bytes 131072
  36.6 0.6 %copy.12 = f32[8,256]{1,0:T(8,128)} copy(f32[8,256]{1,0:T(8,128)S(1)} %get-tuple-element.10) | data formatting | bytes 16384
Async XLA Ops:
  2.1 3.4 %copy-start = (bf16[8,1,256,2048]{3,2,1,0:T(8,128)(2,1)S(1)}, bf16[8,1,256,2048]{3,2,1,0:T(8,128)(2,1)}, u32[]{:S(2)}) copy-start(bf16[8,1,256,2048]{3,2,1,0:T(8,128)(2,1)} %in_plane.1) | copy-start | bytes 25165828
  5.5 0.9 %copy-start.1 = (f32[8,8,512]{2,1,0:T(8,128)S(1)}, f32[8,8,512]{2,1,0:T(8,128)}, u32[]{:S(2)}) copy-start(f32[8,8,512]{2,1,0:T(8,128)} %measured.1) | copy-start | bytes 393220
  6.4 0.8 %copy-start.2 = (f32[8,1,5,2,8]{4,3,2,1,0:T(2,128)S(1)}, f32[8,1,5,2,8]{4,3,2,1,0:T(2,128)}, u32[]{:S(2)}) copy-start(f32[8,1,5,2,8]{4,3,2,1,0:T(2,128)} %tiles.1) | copy-start | bytes 7684
  7.2 0.7 %copy-start.3 = (f32[8,256]{1,0:T(8,128)S(1)}, f32[8,256]{1,0:T(8,128)}, u32[]{:S(2)}) copy-start(f32[8,256]{1,0:T(8,128)} %volume.1) | copy-start | bytes 24580

commit v2 on v1

--- a/solution.py
+++ b/solution.py
@@ -16,7 +16,7 @@
 WEIGHT_MAX = 0.0099487305
 VOLUME_MAX = 2.0
 HALF_CODE = 32500.0
-CHUNKS = 4
+CHUNKS = 2
 
 
 def each(count, fn):
@@ -29,12 +29,13 @@
 
 def kernel(
     cfg,
-    volume, measured, in_plane, bands, counts, tiles,
+    volume_in, measured_in, in_plane, bands_in, counts_in, tiles_in,
     new_volume, residual,
+    volume, measured, bands, counts, tiles,
     wide, rows_t, bd_raw, bd_mean, tw, proj,
     meas_send, meas_recv, half_own, half_send, half_recv,
     code_send, code_recv, gather, res_all, res_wide, acc, x_send, x_recv,
-    w_sem, ms_s, ms_r, f_s, f_r, q_s, q_r, r_s, r_r, p_s, p_r, x_s, x_r,
+    in_sem, w_sem, ms_s, ms_r, f_s, f_r, q_s, q_r, r_s, r_r, p_s, p_r, x_s, x_r,
 ):
     slabs, angs, span, angles, zs, cw, chunks, strip = cfg
     me = lax.axis_index("slab")
@@ -94,6 +95,14 @@
     def others(count, mine, fn):
         each(count - 1, lambda i: fn(lax.rem(mine + i + 1, count)))
 
+    small = [
+        pltpu.make_async_copy(src, dst, in_sem.at[i])
+        for i, (src, dst) in enumerate(
+            ((bands_in, bands), (counts_in, counts), (tiles_in, tiles), (measured_in, measured), (volume_in, volume))
+        )
+    ]
+    for copy in small:
+        copy.start()
     for k in range(chunks):
         load(k).start()
 
@@ -109,11 +118,14 @@
     others(angs, ang, lambda d: pl.semaphore_signal(barrier, inc=1, device_id={"ang": d}, device_id_type=MESH))
     pl.semaphore_signal(barrier, inc=1, device_id={"rep": other}, device_id_type=MESH)
 
+    for copy in small:
+        copy.wait()
+
     def fill(d):
         for a in range(angles):
             meas_send[d, a : a + 1, LANES : LANES + strip] = measured[a, pl.ds(d * 2 + rep, 1), :]
-            first = bands[a, 0, 0]
-            count = counts[a, 0]
+            first = bands[0, 0, a]
+            count = counts[0, a]
             listed = jnp.where((d >= first) & (d < first + count), F32(1), F32(0))
             slot = jnp.clip(d - first, 0, tiles.shape[2] - 1)
             rows_t[0, d, a : a + 1, 0:zs] = tiles[a, 0, slot, pl.ds(rep, 1), :] * listed
@@ -154,6 +166,8 @@
     def project(k):
         load(k).wait()
         for a in range(angles):
+            if a == angles // 2 and k > 0:
+                scatter(k - 1)
             got = jnp.dot(left, wide[k, a], preferred_element_type=F32)
             proj[a * zs : (a + 1) * zs, :] = got[0:zs]
             half_own[k, nrow + a : nrow + a + 1, :] = got[zs : zs + 1]
@@ -248,12 +262,14 @@
         acc[0:zs, :] = update
         acc[zs:, :] = sums
 
-    stages = (project, scatter, solve, relay, back)
-    lags = (0, 1, 2, 3, 4)
-    for step in range(chunks + lags[-1]):
-        for stage, lag in zip(stages, lags):
-            if 0 <= step - lag < chunks:
-                stage(step - lag)
+    for k in range(chunks):
+        project(k)
+    scatter(chunks - 1)
+    for k in range(chunks):
+        solve(k)
+    for k in range(chunks):
+        relay(k)
+        back(k)
 
     x_send[...] = acc[...]
     others(angs, ang, lambda to: x_copy(to, ang).start())
@@ -286,20 +302,23 @@
     chunks = CHUNKS
     cw = width // chunks
     strip = measured.shape[2]
+    bands, counts = pair_bands.transpose(2, 1, 0), pair_counts.T
     cfg = (slabs, angs, span, angles, zs, cw, chunks, strip)
     nrow, nz = slabs * ROWS, angles * zs
     dma = pltpu.SemaphoreType.DMA
     vmem = pl.BlockSpec(memory_space=pltpu.VMEM)
-    smem = pl.BlockSpec(memory_space=pltpu.SMEM)
+    hbm = pl.BlockSpec(memory_space=pltpu.HBM)
     new_volume, residual = pl.pallas_call(
         functools.partial(kernel, cfg),
-        out_shape=(
-            jax.ShapeDtypeStruct((zs, xy), F32),
-            jax.ShapeDtypeStruct((angles, width), F32),
-        ),
-        in_specs=[vmem, vmem, pl.BlockSpec(memory_space=pl.ANY), smem, smem, vmem],
+        out_shape=(pltpu.VMEM((zs, xy), F32), pltpu.VMEM((angles, width), F32)),
+        in_specs=[hbm] * 6,
         out_specs=(vmem, vmem),
         scratch_shapes=[
+            pltpu.VMEM(volume.shape, F32),
+            pltpu.VMEM(measured.shape, F32),
+            pltpu.SMEM(bands.shape, jnp.int32),
+            pltpu.SMEM(counts.shape, jnp.int32),
+            pltpu.VMEM(pair_weight_tiles.shape, F32),
             pltpu.VMEM((chunks, angles, xy, cw), BF16),
             pltpu.VMEM((2, slabs, ROWS, LANES), F32),
             pltpu.VMEM((2 * nrow, nz), F32),
@@ -319,7 +338,7 @@
             pltpu.VMEM((2 * zs, xy), F32),
             pltpu.VMEM((2 * zs, xy), F32),
             pltpu.VMEM((angs, 2 * zs, xy), F32),
-            dma((chunks,)),
+            dma((5,)), dma((chunks,)),
             dma((slabs,)), dma((slabs,)),
             dma((chunks,)), dma((chunks,)),
             dma((chunks, slabs)), dma((chunks, slabs)),
@@ -328,12 +347,12 @@
             dma((angs,)), dma((angs,)),
         ],
         compiler_params=pltpu.CompilerParams(
-            collective_id=0, has_side_effects=True, vmem_limit_bytes=40 * 1024 * 1024
+            collective_id=0, has_side_effects=True, vmem_limit_bytes=60 * 1024 * 1024
         ),
         cost_estimate=pl.CostEstimate(
             flops=8 * angles * zs * xy * width, bytes_accessed=2 * angles * xy * width, transcendentals=0
         ),
-    )(volume, measured, in_plane, pair_bands, pair_counts, pair_weight_tiles)
+    )(volume, measured, in_plane, bands, counts, pair_weight_tiles)
     return new_volume, residual.reshape(angles, 1, width)
 
 

time: 37.5 us -> 25.9 us (0.69)
  local copies, waits for them, and re-layouts: 8.54 us -> 1.3 us
  Pallas kernels: 28 us -> 23.8 us
    unnamed x12 -> x2, local copies, waits for them, and re-layouts: 8.54 us -> 1.3 us
    pallas_call x1, Pallas kernels: 28 us -> 23.8 us  [body(): pl.pallas_call(functools.partial(kernel, cfg), out_shape=(pltpu.VMEM((zs,...]
where the time goes in v2:
time: 25.9 us; the launch traced here: 25.7 us
  Pallas kernels  23.8 us (92%)
  local copies, waits for them, and re-layouts  1.3 us (5%)
  between operations  0.64 us (2%)
    pallas_call x1, Pallas kernels, body(): pl.pallas_call(functools.partial(kernel, cfg), out_shape=(pltpu.VMEM((zs,...  23.8 us
    unnamed x2, local copies, waits for them, and re-layouts  1.3 us

profile of v2, /device:TPU:0, one launch (start us, length us, event | category | flops | bytes accessed | tf_op | source)
XLA Modules:
  0.0 25.7 jit_solution(7732852521059934052)
XLA Ops:
  0.6 23.8 %shard_map.77 = (f32[8,256]{1,0:T(8,128)S(1)}, f32[8,2048]{1,0:T(8,128)S(1)}) custom-call(f32[8,256]{1,0:T(8,128)} %volume_in.1, f32[8,8,512]{2,1,0:T(8,128)} %measured_in.1, bf16[8,1,256,2048]{3,2,1,0:T(8,128)(2,1)} %in_plane.1, s32[5,1,8]{2,1,0:T(1,128)} %bitcast.4, s32[1,8]{1,0:T(1,128)} %bitcast.5, f32[8,1,5,2,8]{4,3,2,1,0:T(2,128)} %tiles_in.1), custom_call_target="tpu_custom_call" | custom-call | flops 268435456 | bytes 8388608 | tf_op jit(solution)/shard_map/pallas_call | solution.py:311
  24.4 0.6 %copy.10 = f32[8,256]{1,0:T(8,128)} copy(f32[8,256]{1,0:T(8,128)S(1)} %get-tuple-element.8) | data formatting | bytes 16384
  25.0 0.7 %copy.8 = f32[8,1,2048]{2,1,0:T(1,128)} copy(f32[8,1,2048]{2,0,1:T(8,128)S(1)} %bitcast.3) | data formatting | bytes 131072

commit v3 on v2

--- a/solution.py
+++ b/solution.py
@@ -82,9 +82,9 @@
     def x_copy(to, slot):
         return remote(x_send, x_recv.at[slot], x_s.at[to], x_r.at[slot], {"ang": to})
 
-    def near(fn):
+    def near(fn, far=False):
         def one(i):
-            d = me + (span - i // 2) * (1 - 2 * (i % 2))
+            d = me + (span - i // 2 if far else 1 + i // 2) * (1 - 2 * (i % 2))
 
             @pl.when((d >= 0) & (d < slabs))
             def _():
@@ -188,7 +188,7 @@
             code_send[k, d] = code.astype(jnp.int32).astype(jnp.int16)
             code_copy(k, d, me).start()
 
-        near(send)
+        near(send, True)
 
     def wide_weight(s):
         return jnp.concatenate([meas_recv[s, :, 0:LANES]] * (cw // LANES), axis=1)
@@ -225,7 +225,7 @@
             res = jnp.where(lax.broadcasted_iota(jnp.int32, res.shape, 0) < angles, res, 0.0)
         residual[:, cols(k)] = res[0:angles]
         gather[k, 0, me] = jnp.concatenate([res[:, : cw // 2], res[:, cw // 2 :]], axis=0).astype(BF16)
-        near(lambda d: res_copy(k, d, me).start())
+        near(lambda d: res_copy(k, d, me).start(), True)
         pass_copy(k, me).start()
 
     def relay(k):

time: 25.9 us -> 25.9 us (level)
  no operation moved by 1% of the time
where the time goes in v3:
time: 25.9 us; the launch traced here: 25.7 us
  Pallas kernels  23.8 us (92%)
  local copies, waits for them, and re-layouts  1.3 us (5%)
  between operations  0.64 us (2%)
    pallas_call x1, Pallas kernels, body(): pl.pallas_call(functools.partial(kernel, cfg), out_shape=(pltpu.VMEM((zs,...  23.8 us
    unnamed x2, local copies, waits for them, and re-layouts  1.3 us

profile of v3, /device:TPU:0, one launch (start us, length us, event | category | flops | bytes accessed | tf_op | source)
XLA Modules:
  0.0 25.7 jit_solution(523065697826254095)
XLA Ops:
  0.6 23.8 %shard_map.77 = (f32[8,256]{1,0:T(8,128)S(1)}, f32[8,2048]{1,0:T(8,128)S(1)}) custom-call(f32[8,256]{1,0:T(8,128)} %volume_in.1, f32[8,8,512]{2,1,0:T(8,128)} %measured_in.1, bf16[8,1,256,2048]{3,2,1,0:T(8,128)(2,1)} %in_plane.1, s32[5,1,8]{2,1,0:T(1,128)} %bitcast.4, s32[1,8]{1,0:T(1,128)} %bitcast.5, f32[8,1,5,2,8]{4,3,2,1,0:T(2,128)} %tiles_in.1), custom_call_target="tpu_custom_call" | custom-call | flops 268435456 | bytes 8388608 | tf_op jit(solution)/shard_map/pallas_call | solution.py:311
  24.4 0.6 %copy.10 = f32[8,256]{1,0:T(8,128)} copy(f32[8,256]{1,0:T(8,128)S(1)} %get-tuple-element.8) | data formatting | bytes 16384
  25.0 0.7 %copy.8 = f32[8,1,2048]{2,1,0:T(1,128)} copy(f32[8,1,2048]{2,0,1:T(8,128)S(1)} %bitcast.3) | data formatting | bytes 131072
